TPU v7x, 32 devices: a whole 2x2x4 slice. The times are simulated.
32 devices in a mesh: groups: 2 (over x), row: 8 (over z, y), col: 2 (over core).
Axes of the slice: x: 2, y: 2, z: 4, core: 2. Of those that a mesh axis runs over, the one named last changes fastest.
Arguments:
- activations: bfloat16 [4096, 8192], P(('groups', 'row'), 'col'), parts along dimension 0, may hold values from -6 to 6
- output_gradient: bfloat16 [4096, 16384], P(('groups', 'col'), 'row'), parts along dimension 0, may hold values from -6 to 6
- frozen_weight: bfloat16 [8192, 16384], P('col', 'row'), may hold values from -0.046875 to 0.046875
- adapter_down_maps: bfloat16 [64, 16, 8192], P(None, None, ('col', 'row')), may hold values from -0.25 to 0.25
- adapter_up_maps: bfloat16 [64, 16, 16384], P(None, None, 'row'), may hold values from -0.046875 to 0.046875
- adapter_of_block: int32 [32], P('groups'), parts along dimension 0, may hold values from 0 to 63
- adapter_grad_slot: int32 [64], replicated, may hold values from 0 to 63, each once
Outputs:
- input_grad: bfloat16 [4096, 8192], P(('groups', 'row'), 'col'), parts along dimension 0
- down_grad: bfloat16 [128, 16, 8192], P(('groups', 'row'), None, 'col'), parts along dimension 0
- up_grad: bfloat16 [128, 16, 16384], P(('groups', 'col'), None, 'row'), parts along dimension 0
There are 2 independent parts, one for each index of `groups`. A program takes and returns all parts, laid end to end along the dimension named above; an argument that names none is the same for every part. Nothing has to cross between parts.
Inputs may be any that keep to these rules, and one draw needn't show every extreme that they name: adapter_grad_slot holds every number below 64 once; slot s belongs to the adapter a with adapter_grad_slot[a] = s.
All inputs are finite; a program needn't handle non-finite values.
Results may differ from a plain program's by a relative error of at most 0.015.
Values may be sent and summed in bfloat16 or wider, within the bound.
A program may use at most 192 MiB of HBM per device.

v0:
```python
import jax
import jax.numpy as jnp
from jax import lax
from jax.sharding import PartitionSpec as P

BLOCK = 128


SCALE = 2.0
HIGH_PRECISION = lax.Precision.HIGHEST


def shards(
    activations,
    output_gradient,
    frozen_weight,
    adapter_down_maps,
    adapter_up_maps,
    adapter_of_block,
    adapter_grad_slot,
):
    n_row = lax.axis_size("row")
    n_col = lax.axis_size("col")
    index_of_row = lax.axis_index("row")
    col_index = lax.axis_index("col")
    adapter_list = adapter_down_maps.shape[0]
    rank_width = adapter_down_maps.shape[1]
    token_slab = adapter_down_maps.shape[2]
    width_out = output_gradient.shape[1]
    half_blocks = output_gradient.shape[0] // BLOCK
    blocks = half_blocks * n_col
    every_token = blocks * BLOCK
    dy_panel = lax.all_gather(output_gradient, "col", axis=0, tiled=True)
    x_columns = lax.all_to_all(activations, "row", split_axis=1, concat_axis=0, tiled=True)
    x_blocks = x_columns.reshape(blocks, BLOCK, token_slab)
    selected_down = adapter_down_maps[adapter_of_block]
    selected_up = adapter_up_maps[adapter_of_block]
    hidden_part = jnp.einsum(
        "btd,brd->btr", x_blocks, selected_down, preferred_element_type=jnp.float32
    )
    own_dy = output_gradient.reshape(half_blocks, BLOCK, width_out)
    own_up = lax.dynamic_slice_in_dim(selected_up, col_index * half_blocks, half_blocks, 0)
    back_own = jnp.einsum("bto,bro->btr", own_dy, own_up, preferred_element_type=jnp.float32)
    back_zero = jnp.zeros((blocks, BLOCK, rank_width), jnp.float32)
    back_part = lax.dynamic_update_slice_in_dim(back_zero, back_own, col_index * half_blocks, 0)
    hidden, back_sum = lax.psum((hidden_part, back_part), ("row", "col"))
    back = SCALE * back_sum
    hidden_low = hidden.astype(jnp.bfloat16)
    backward_low_rank = back.astype(jnp.bfloat16)
    adapter_token_slab = jnp.einsum(
        "efs,esl->efl", backward_low_rank, selected_down, preferred_element_type=jnp.float32
    )
    adapter_token_slab = adapter_token_slab.reshape(every_token, token_slab)
    partial_term = lax.dot_general(
        dy_panel, frozen_weight, (((1,), (1,)), ((), ())), preferred_element_type=jnp.float32
    )
    present_value = lax.dynamic_slice_in_dim(partial_term, index_of_row * token_slab, token_slab, 1)
    input_grad = lax.psum_scatter(
        lax.dynamic_update_slice_in_dim(
            partial_term, present_value + adapter_token_slab, index_of_row * token_slab, 1
        ).astype(jnp.bfloat16),
        "row",
        scatter_dimension=0,
        tiled=True,
    )
    slot_of_block = adapter_grad_slot[adapter_of_block]
    down_parts = jnp.einsum(
        "btr,btd->brd", backward_low_rank, x_blocks, preferred_element_type=jnp.float32
    )
    per_row = adapter_list // n_row
    own_slots = index_of_row * per_row + jnp.arange(per_row, dtype=jnp.int32)
    choose_own = (slot_of_block[None, :] == own_slots[:, None]).astype(jnp.float32)
    summed = jnp.einsum(
        "sb,brd->srd",
        choose_own,
        lax.all_gather(down_parts.astype(jnp.bfloat16), "row", axis=2, tiled=True).astype(
            jnp.float32
        ),
        precision=HIGH_PRECISION,
    )
    down_grad = (summed / BLOCK).astype(jnp.bfloat16)
    own_hidden = lax.dynamic_slice_in_dim(hidden_low, col_index * half_blocks, half_blocks, 0)
    own_cotangent = output_gradient.reshape(half_blocks, BLOCK, width_out)
    up_parts = jnp.einsum(
        "btr,bto->bro", own_hidden, own_cotangent, preferred_element_type=jnp.float32
    )
    every_block = lax.all_gather(up_parts.astype(jnp.bfloat16), "col", axis=0, tiled=True).astype(
        up_parts.dtype
    )
    per_col = adapter_list // n_col
    col_slots = col_index * per_col + jnp.arange(per_col, dtype=jnp.int32)
    choose_col = (slot_of_block[None, :] == col_slots[:, None]).astype(jnp.float32)
    up_grad = (
        SCALE / BLOCK * jnp.einsum("sb,bro->sro", choose_col, every_block, precision=HIGH_PRECISION)
    ).astype(jnp.bfloat16)
    return (input_grad, down_grad, up_grad)


def solution(mesh):
    in_specs = (
        P(("groups", "row"), "col"),
        P(("groups", "col"), "row"),
        P("col", "row"),
        P(None, None, ("col", "row")),
        P(None, None, "row"),
        P("groups"),
        P(),
    )
    out_specs = (
        P(("groups", "row"), "col"),
        P(("groups", "row"), None, "col"),
        P(("groups", "col"), None, "row"),
    )
    return jax.shard_map(shards, mesh=mesh, in_specs=in_specs, out_specs=out_specs, check_vma=False)
```

profile of v0, /device:TPU:0, one launch (start us, length us, event | category | flops | bytes accessed | tf_op | source)
XLA Modules:
  0.0 500.2 jit_solution(2329222168873854224)
XLA Ops:
  8.0 0.0 all-reduce.3.cloned.1.call-start
  8.1 0.7 compare_select_fusion
  8.8 2.8 gather_fusion
  11.6 3.4 fusion.2
  15.0 0.7 copy-done.7
  15.7 0.0 all-gather.4.cloned.1.call-start
  15.8 0.5 all-gather.4.cloned.1.call-update
  16.3 0.4 copy-done.5
  16.7 2.4 copy.20
  19.1 7.3 %all-to-all-start = ((bf16[256,8,512]{0,2,1:T(8,128)(2,1)}), bf16[256,8,512]{0,2,1:T(8,128)(2,1)S(1)}, u32[]{:S(2)}, u32[]{:S(2)}) async-start(bf16[256,8,512]{0,2,1:T(8,128)(2,1)} %bitcast.31), calls=%async_computation.1 | async-start | bytes 4194304 | tf_op jit(solution)/shard_map/all_to_all | solution.py:34
  26.4 0.0 all-gather.8.cloned.1.call-start
  26.4 0.6 gather_fusion.1
  27.0 48.7 %all-to-all-done = bf16[256,8,512]{0,2,1:T(8,128)(2,1)S(1)} async-done(((bf16[256,8,512]{0,2,1:T(8,128)(2,1)}), bf16[256,8,512]{0,2,1:T(8,128)(2,1)S(1)}, u32[]{:S(2)}, u32[]{:S(2)}) %all-to-all-start) | async-done | bytes 2097184 | tf_op jit(solution)/shard_map/all_to_all | solution.py:34
  75.7 1.3 copy-done.4
  77.0 2.9 copy.21
  79.9 0.6 convolution_bitcast_fusion
  80.5 60.2 %all-reduce.4 = bf16[16,128,16]{1,2,0:T(8,128)(2,1)S(1)} all-reduce(f32[16,128,16]{1,2,0:T(8,128)S(1)} %convolution_bitcast_fusion), channel_id=1, replica_groups=mesh['groups'=2,'row'=8,'col'=2] {'row','col'}, use_global_device_ids=true, to_apply=%region_2.0 | all-reduce | flops 32768 | bytes 196608 | tf_op jit(solution)/shard_map/psum | solution.py:46
  140.8 3.6 convolution_convert_fusion
  144.5 0.0 all-gather.6.cloned.1.call-start
  144.5 3.7 fusion.5
  148.2 1.1 convolution_convert_fusion.1
  149.3 0.2 reduce-scatter.2.cloned.1.call-start
  149.6 43.9 %fusion.18 = f32[2048,4096]{1,0:T(8,128)} fusion(bf16[2048,2048]{1,0:T(8,128)(2,1)} %all-gather.4.cloned.1.call-done, bf16[4096,2048]{1,0:T(8,128)(2,1)} %param.9), kind=kOutput, calls=%fused_computation.35 | convolution fusion | flops 34359738368 | bytes 58720256 | tf_op jit(solution)/shard_map/dot_general | solution.py:54
  193.5 4.8 constant_dynamic-update-slice_fusion
  198.3 17.4 %convert_element_type.26 = bf16[2048,4096]{1,0:T(8,128)(2,1)} convert(f32[2048,4096]{1,0:T(8,128)} %constant_dynamic-update-slice_fusion) | non-fusion elementwise | flops 8388608 | bytes 50331648 | tf_op jit(solution)/shard_map/convert_element_type | solution.py:61
  215.7 0.6 copy-done.2
  216.3 0.7 gather_fusion.2
  217.1 2.8 multiply_convert_fusion
  219.8 2.5 copy.25
  222.3 3.9 fusion
  226.3 1.6 copy.24
  227.8 264.8 %reduce-scatter.2.cloned.1.call-done = bf16[256,4096]{1,0:T(8,128)(2,1)} async-done(((bf16[2048,4096]{1,0:T(8,128)(2,1)}), bf16[256,4096]{1,0:T(8,128)(2,1)}) %reduce-scatter.2.cloned.1.call-update) | async-done | bytes 2097168 | tf_op jit(solution)/shard_map/reduce_scatter | solution.py:58
  (24 shorter events, 0.2 us)
Async XLA Ops:
  8.0 18.4 %copy-start = (bf16[64,16,512]{2,1,0:T(8,128)(2,1)S(1)}, bf16[64,16,512]{2,1,0:T(8,128)(2,1)}, u32[]{:S(2)}) copy-start(bf16[64,16,512]{2,1,0:T(8,128)(2,1)} %param.10) | copy-start | bytes 3145732
  8.0 136.5 %all-reduce.3.cloned.1.call-start = ((), (), s32[]{:S(2)}) async-start(), calls=%async_computation.3 | async-start | bytes 262144 | tf_op jit(solution)/shard_map/psum | solution.py:46
  15.0 0.7 copy-start.7
  15.0 1.7 copy-start.5
  15.7 133.9 %all-gather.4.cloned.1.call-start = ((), (), s32[]{:S(2)}) async-start(), calls=%async_computation.2 | async-start | bytes 12582912 | tf_op jit(solution)/shard_map/all_gather | solution.py:33
  19.1 56.6 %all-to-all-start = ((bf16[256,8,512]{0,2,1:T(8,128)(2,1)}), bf16[256,8,512]{0,2,1:T(8,128)(2,1)S(1)}, u32[]{:S(2)}, u32[]{:S(2)}) async-start(bf16[256,8,512]{0,2,1:T(8,128)(2,1)} %bitcast.31), calls=%async_computation.1 | async-start | bytes 4194304 | tf_op jit(solution)/shard_map/all_to_all | solution.py:34
  26.4 190.7 %all-gather.8.cloned.1.call-start = ((), (), s32[]{:S(2)}) async-start(), calls=%async_computation.6 | async-start | bytes 1572864 | tf_op jit(solution)/shard_map/all_gather | solution.py:87
  75.7 1.3 copy-start.4
  144.5 77.9 %all-gather.6.cloned.1.call-start = ((), (), s32[]{:S(2)}) async-start(), calls=%async_computation.5 | async-start | bytes 2359296 | tf_op jit(solution)/shard_map/all_gather | solution.py:76
  144.5 3.7 copy-start.6
  149.3 343.2 %reduce-scatter.2.cloned.1.call-start = ((), (), s32[]{:S(2)}) async-start(), calls=%async_computation.4 | async-start | bytes 18874368 | tf_op jit(solution)/shard_map/reduce_scatter | solution.py:58
  149.6 43.9 %copy-start.3 = (f32[16,128,512]{2,1,0:T(8,128)S(1)}, f32[16,128,512]{2,1,0:T(8,128)}, u32[]{:S(2)}) copy-start(f32[16,128,512]{2,1,0:T(8,128)} %fusion.5) | copy-start | bytes 12582916
  215.7 0.7 copy-start.2
  217.1 275.5 %copy-start.1 = (bf16[64,16,512]{2,1,0:T(8,128)(2,1)S(1)}, bf16[64,16,512]{2,1,0:T(8,128)(2,1)}, u32[]{:S(2)}) copy-start(bf16[64,16,512]{2,1,0:T(8,128)(2,1)} %param.10) | copy-start | bytes 3145732
Sparse Core Ops, SparseCore 0:
  15.8 112.7 all-reduce.2
Sparse Core Ops, SparseCore 1:
  17.7 22.4 all-gather.3
  144.5 6.2 all-gather.7
  152.7 51.7 all-gather.5
  215.8 276.7 reduce-scatter.1
where the time goes:
time: 501 us; the launch traced here: 500 us
  waiting for transfers between devices  314 us (63%)
  matrix products  63.1 us (13%)
  blocking collectives  60.2 us (12%)
  other arithmetic  22.9 us (5%)
  local copies, waits for them, and re-layouts  16.4 us (3%)
  between operations  15.8 us (3%)
  starting transfers between devices  7.67 us (2%)
    reduce_scatter x1, waiting for transfers between devices, shards(): lax.psum_scatter(lax.dynamic_update_slice_in_dim(partial_term, present_va...  265 us
    psum x1, blocking collectives, shards(): hidden, back_sum = lax.psum((hidden_part, back_part), ('row', 'col'))  60.2 us
    all_to_all x1, waiting for transfers between devices, shards(): lax.all_to_all(activations, 'row', split_axis=1, concat_axis=0, tiled=True)  48.7 us
    dot_general x1, matrix products, shards(): lax.dot_general(dy_panel, frozen_weight, (((1,), (1,)), ((), ())), prefer...  43.9 us
    convert_element_type x1, other arithmetic, shards(): input_grad = lax.psum_scatter(lax.dynamic_update_slice_in_dim(partial_ter...  17.4 us
  transfers between devices with their start and end apart: 6, of which 2 were waited for; matrix products, arithmetic and copies ran while one was open for 18% of the time, Pallas kernels for 0%

commit v1 on v0

--- a/solution.py
+++ b/solution.py
@@ -10,7 +10,7 @@
 HIGH_PRECISION = lax.Precision.HIGHEST
 
 
-def shards(
+def general_shards(
     activations,
     output_gradient,
     frozen_weight,
@@ -96,6 +96,158 @@
     return (input_grad, down_grad, up_grad)
 
 
+LINE_ORDER = ((3, 2, 1, 0), (3, 2, 0, 1), (0, 1, 3, 2), (0, 1, 2, 3))
+PIECES = 2
+
+
+def grid_shards(
+    activations,
+    output_gradient,
+    frozen_weight,
+    adapter_down_maps,
+    adapter_up_maps,
+    adapter_of_block,
+    adapter_grad_slot,
+):
+    n_row = lax.axis_size("row")
+    n_col = lax.axis_size("col")
+    row = lax.axis_index("row")
+    col = lax.axis_index("col")
+    z, y = row // 2, row % 2
+    adapters, rank, slab = adapter_down_maps.shape
+    width_out = output_gradient.shape[1]
+    features = activations.shape[1]
+    own_tokens = activations.shape[0]
+    own_blocks = own_tokens // BLOCK
+    half_tokens = output_gradient.shape[0]
+    half_blocks = half_tokens // BLOCK
+    blocks = half_blocks * n_col
+    order = jnp.array(LINE_ORDER, jnp.int32)[z]
+    other_core = [(i, (i + 1) % n_col) for i in range(n_col)]
+    other_y = [(i, i ^ 1) for i in range(n_row)]
+
+    chunk = half_tokens // 2
+    first = jnp.where(z < 2, 1, 0)
+    mine_first = col == first
+    own_pairs, got_pairs = [], []
+    for i in range(2):
+        place = jnp.where(mine_first, order[i], order[2 + i]) - 2 * col
+        own = lax.dynamic_slice_in_dim(output_gradient, place * chunk, chunk, 0)
+        own_pairs.append(own)
+        got_pairs.append(lax.ppermute(own, "col", other_core))
+    rows_of = [jnp.where(mine_first, own_pairs[i], got_pairs[i]) for i in range(2)]
+    rows_of += [jnp.where(mine_first, got_pairs[i], own_pairs[i]) for i in range(2)]
+
+    def product(p, which_y, piece):
+        part = lax.dynamic_slice_in_dim(rows_of[p], which_y * own_tokens, own_tokens, 0)
+        width = features // PIECES
+        weight = frozen_weight[piece * width : (piece + 1) * width]
+        return lax.dot_general(
+            part, weight, (((1,), (1,)), ((), ())), preferred_element_type=jnp.float32
+        ).astype(jnp.bfloat16)
+
+    def wide(v):
+        return v.astype(jnp.float32)
+
+    arrived = {}
+    kept = {}
+    for p in range(4):
+        for piece in range(PIECES):
+            arrived[p, piece] = lax.ppermute(product(p, 1 - y, piece), "row", other_y)
+        for piece in range(PIECES):
+            kept[p, piece] = product(p, y, piece)
+
+    right = {k: [(r, r + 2) for r in range(2 * k)] for k in (1, 2, 3)}
+    left = {k: [(n_row - 1 - s, n_row - 1 - d) for s, d in right[k]] for k in (1, 2, 3)}
+    totals = []
+    for piece in range(PIECES):
+        s = [wide(kept[p, piece]) + wide(arrived[p, piece]) for p in range(4)]
+        r1 = lax.ppermute(s[0].astype(jnp.bfloat16), "row", right[1])
+        l1 = lax.ppermute(s[0].astype(jnp.bfloat16), "row", left[1])
+        r2 = jnp.where(z == 0, s[1], s[0]) + wide(r1)
+        l2 = jnp.where(z == 3, s[1], s[0]) + wide(l1)
+        r2 = lax.ppermute(r2.astype(jnp.bfloat16), "row", right[2])
+        l2 = lax.ppermute(l2.astype(jnp.bfloat16), "row", left[2])
+        r3 = jnp.where(z == 1, s[1], s[2]) + wide(r2)
+        l3 = jnp.where(z == 2, s[1], s[2]) + wide(l2)
+        r3 = lax.ppermute(r3.astype(jnp.bfloat16), "row", right[3])
+        l3 = lax.ppermute(l3.astype(jnp.bfloat16), "row", left[3])
+        totals.append((s[3], r3, l3))
+
+    x_blocks = activations.reshape(own_blocks, BLOCK, features)
+    own_dy = output_gradient.reshape(half_blocks, BLOCK, width_out)
+    half_adapters = lax.dynamic_slice_in_dim(adapter_of_block, col * half_blocks, half_blocks, 0)
+    down_rows = lax.all_to_all(
+        adapter_down_maps[adapter_of_block], "row", split_axis=0, concat_axis=2, tiled=True
+    )
+    back_half = jnp.einsum(
+        "bro,bto->brt", adapter_up_maps[half_adapters], own_dy, preferred_element_type=jnp.float32
+    )
+    back_every = lax.dynamic_update_slice_in_dim(
+        jnp.zeros((blocks, rank, BLOCK), jnp.float32), back_half, col * half_blocks, 0
+    )
+    back_parts = lax.all_to_all(
+        back_every.reshape(n_row, own_blocks * rank, BLOCK), "row", split_axis=0, concat_axis=0
+    )
+    back_own = back_parts.sum(0).reshape(own_blocks, rank, BLOCK)
+    hidden_own = jnp.einsum(
+        "brd,btd->brt", down_rows, x_blocks, preferred_element_type=jnp.float32
+    )
+    both = jnp.concatenate([hidden_own, back_own])
+    both = both + lax.ppermute(both, "col", other_core)
+    hidden_low = both[:own_blocks].astype(jnp.bfloat16)
+    back_low = (SCALE * both[own_blocks:]).astype(jnp.bfloat16)
+    hidden_all = lax.all_gather(hidden_low, "row", axis=0, tiled=True)
+
+    lora = jnp.einsum("brt,brd->btd", back_low, down_rows, preferred_element_type=jnp.float32)
+    lora = lora.reshape(own_tokens, features)
+    width = features // PIECES
+    input_grad = jnp.concatenate(
+        [
+            (
+                s + wide(r) + wide(l) + lora[:, i * width : (i + 1) * width]
+            ).astype(jnp.bfloat16)
+            for i, (s, r, l) in enumerate(totals)
+        ],
+        axis=1,
+    )
+
+    slot_of_block = adapter_grad_slot[adapter_of_block]
+    down_parts = jnp.einsum(
+        "brt,btd->brd", back_low, x_blocks, preferred_element_type=jnp.float32
+    ).astype(jnp.bfloat16)
+    down_all = lax.all_gather(down_parts, "row", axis=0, tiled=True)
+    per_row = adapters // n_row
+    own_slots = row * per_row + jnp.arange(per_row, dtype=jnp.int32)
+    choose_own = (slot_of_block[None, :] == own_slots[:, None]).astype(jnp.bfloat16)
+    down_grad = jnp.einsum("sb,brd->srd", choose_own, down_all, preferred_element_type=jnp.float32)
+    down_grad = (down_grad / BLOCK).astype(jnp.bfloat16)
+
+    hidden_half = lax.dynamic_slice_in_dim(hidden_all, col * half_blocks, half_blocks, 0)
+    up_parts = jnp.einsum(
+        "brt,bto->bro", hidden_half, own_dy, preferred_element_type=jnp.float32
+    ).astype(jnp.bfloat16)
+    up_got = lax.ppermute(up_parts, "col", other_core)
+    per_col = adapters // n_col
+    col_slots = col * per_col + jnp.arange(per_col, dtype=jnp.int32)
+    choose_col = (slot_of_block[None, :] == col_slots[:, None]).astype(jnp.bfloat16)
+    half_slots = jnp.concatenate(
+        [
+            lax.dynamic_slice_in_dim(choose_col, col * half_blocks, half_blocks, 1),
+            lax.dynamic_slice_in_dim(choose_col, (1 - col) * half_blocks, half_blocks, 1),
+        ],
+        axis=1,
+    )
+    up_grad = jnp.einsum(
+        "sb,bro->sro",
+        half_slots,
+        jnp.concatenate([up_parts, up_got]),
+        preferred_element_type=jnp.float32,
+    )
+    up_grad = (SCALE / BLOCK * up_grad).astype(jnp.bfloat16)
+    return (input_grad, down_grad, up_grad)
+
+
 def solution(mesh):
     in_specs = (
         P(("groups", "row"), "col"),
@@ -111,4 +263,6 @@
         P(("groups", "row"), None, "col"),
         P(("groups", "col"), None, "row"),
     )
+    grid = mesh.shape["row"] == 8 and mesh.shape["col"] == 2
+    shards = grid_shards if grid else general_shards
     return jax.shard_map(shards, mesh=mesh, in_specs=in_specs, out_specs=out_specs, check_vma=False)

time: 501 us -> 369 us (0.74)
  waiting for transfers between devices: 314 us -> 143 us
  starting transfers between devices: 7.67 us -> 46.4 us
  matrix products: 63.1 us -> 97.5 us
  blocking collectives: 60.2 us -> 31 us
  other arithmetic: 22.9 us -> 13 us
    reduce_scatter x1 -> x0, waiting for transfers between devices: 265 us -> none  [shards(): lax.psum_scatter(lax.dynamic_update_slice_in_dim(partial_term, present_va...]
    ppermute x0 -> x24, waiting for transfers between devices: none -> 140 us  [the longest x8 98.6 us: grid_shards(): arrived[p, piece] = lax.ppermute(product(p, 1 - y, piece), 'row', other_y)]
    psum x1 -> x0, blocking collectives: 60.2 us -> none  [shards(): hidden, back_sum = lax.psum((hidden_part, back_part), ('row', 'col'))]
    all_to_all x1 -> x2, waiting for transfers between devices: 48.7 us -> 3.21 us  [the longest x1 2.34 us: grid_shards(): lax.all_to_all(adapter_down_maps[adapter_of_block], 'row', split_axis=0,...]
    dot_general x8 -> x23, matrix products: 63.1 us -> 97.5 us  [the longest x16 80.7 us: product(): lax.dot_general(part, weight, (((1,), (1,)), ((), ())), preferred_element...]
    ppermute x0 -> x24, starting transfers between devices: none -> 34 us  [the longest x2 9.77 us: grid_shards(): r3 = lax.ppermute(r3.astype(jnp.bfloat16), 'row', right[3])]
    all_gather x0 -> x1, blocking collectives: none -> 31 us  [grid_shards(): hidden_all = lax.all_gather(hidden_low, 'row', axis=0, tiled=True)]
    convert_element_type x1 -> x5, other arithmetic: 17.4 us -> 5.33 us  [the longest x2 3.73 us: grid_shards(): r3 = lax.ppermute(r3.astype(jnp.bfloat16), 'row', right[3])]
  transfers between devices with their start and end apart: 6 -> 27, of which waited for: 2 -> 13; matrix products, arithmetic and copies ran while one was open for 18% -> 30% of each run, Pallas kernels for 0% -> 0%
where the time goes in v1:
time: 369 us; the launch traced here: 365 us
  waiting for transfers between devices  143 us (39%)
  matrix products  97.5 us (26%)
  starting transfers between devices  46.4 us (13%)
  blocking collectives  31 us (8%)
  between operations  17.3 us (5%)
  local copies, waits for them, and re-layouts  17.1 us (5%)
  other arithmetic  13 us (4%)
    ppermute x8, waiting for transfers between devices, grid_shards(): arrived[p, piece] = lax.ppermute(product(p, 1 - y, piece), 'row', other_y)  98.6 us
    dot_general x16, matrix products, product(): lax.dot_general(part, weight, (((1,), (1,)), ((), ())), preferred_element...  80.7 us
    all_gather x1, blocking collectives, grid_shards(): hidden_all = lax.all_gather(hidden_low, 'row', axis=0, tiled=True)  31 us
    ppermute x2, waiting for transfers between devices, grid_shards(): r3 = lax.ppermute(r3.astype(jnp.bfloat16), 'row', right[3])  21.5 us
    ppermute x2, waiting for transfers between devices, grid_shards(): r2 = lax.ppermute(r2.astype(jnp.bfloat16), 'row', right[2])  17.2 us
    ppermute x2, starting transfers between devices, grid_shards(): r3 = lax.ppermute(r3.astype(jnp.bfloat16), 'row', right[3])  9.77 us
  transfers between devices with their start and end apart: 27, of which 13 were waited for; matrix products, arithmetic and copies ran while one was open for 30% of the time, Pallas kernels for 0%

profile of v1, /device:TPU:0, one launch (start us, length us, event | category | flops | bytes accessed | tf_op | source)
XLA Modules:
  0.0 365.5 jit_solution(370134982730736648)
XLA Ops:
  11.5 4.0 %convolution_dynamic-update-slice_fusion = f32[16,16,128]{2,1,0:T(8,128)} fusion(f32[16,16,128]{2,1,0:T(8,128)} %broadcast_in_dim.7, s32[]{:T(128)S(6)} %select_n.152, bf16[8,16,2048]{2,1,0:T(8,128)(2,1)S(1)} %gather_fusion.1, bf16[8,128,2048]{2,1,0:T(8,128)(2,1)} %bitcast.30), kind=kOutput, calls=%fused_computation.78 | convolution fusion | flops 67108864 | bytes 4784132 | tf_op jit(solution)/shard_map/bro,bto->brt/dot_general | solution.py:183
  15.5 7.3 %all-to-all-start.1 = ((f32[8,32,128]{2,1,0:T(8,128)}), f32[8,32,128]{2,1,0:T(8,128)S(1)}, u32[]{:S(2)}, u32[]{:S(2)}) async-start(f32[8,32,128]{2,1,0:T(8,128)} %bitcast.8), calls=%async_computation.1 | async-start | bytes 262144 | tf_op jit(solution)/shard_map/all_to_all | solution.py:189
  30.2 5.1 %all-to-all-start = ((bf16[16,16,512]{2,1,0:T(8,128)(2,1)}), bf16[16,16,512]{2,1,0:T(8,128)(2,1)S(1)}, u32[]{:S(2)}, u32[]{:S(2)}) async-start(bf16[16,16,512]{2,1,0:T(8,128)(2,1)} %gather_fusion), calls=%async_computation | async-start | bytes 524288 | tf_op jit(solution)/shard_map/all_to_all | solution.py:180
  35.4 4.8 %constant_dynamic-slice_fusion.3 = (bf16[512,2048]{1,0:T(8,128)(2,1)}, bf16[512,2048]{1,0:T(8,128)(2,1)}) fusion(bf16[1024,2048]{1,0:T(8,128)(2,1)} %param.9, s32[]{:T(128)S(6)} %select_n.133, s32[]{:T(128)S(6)} %select_n.141), kind=kLoop, calls=%fused_computation.131 | loop fusion | bytes 8388616 | tf_op jit(solution)/shard_map/dynamic_slice | solution.py:135
  47.4 31.0 %all_gather.7 = bf16[16,16,128]{2,1,0:T(8,128)(2,1)S(1)} all-gather(bf16[2,16,128]{2,1,0:T(8,128)(2,1)S(1)} %slice.109), channel_id=1, replica_groups=mesh['groups'=2,'row'=8,'col'=2] {'row'}, dimensions={0}, use_global_device_ids=true | all-gather | bytes 73728 | tf_op jit(solution)/shard_map/all_gather | solution.py:200
  91.9 6.9 %convolution_convert_fusion.11 = bf16[256,2048]{1,0:T(8,128)(2,1)} fusion(bf16[4096,2048]{1,0:T(8,128)(2,1)} %param.10, bf16[512,2048]{1,0:T(8,128)(2,1)S(1)} %get-tuple-element.22, s32[]{:T(128)S(6)} %select_n.137), kind=kOutput, calls=%fused_computation.31 | convolution fusion | flops 2148007936 | bytes 10485764 | tf_op jit(solution)/shard_map/dot_general | solution.py:145
  98.8 3.3 convolution_convert_fusion.3
  104.7 3.3 convolution_convert_fusion.13
  108.0 3.6 convolution_convert_fusion.5
  129.0 15.5 %collective-permute-done.5 = bf16[256,2048]{1,0:T(8,128)(2,1)} collective-permute-done((bf16[256,2048]{1,0:T(8,128)(2,1)}, bf16[256,2048]{1,0:T(8,128)(2,1)}, u32[]{:S(2)}, u32[]{:S(2)}) %collective-permute-start.5) | collective-permute-done | bytes 1048608 | tf_op jit(solution)/shard_map/ppermute | solution.py:156
  144.6 6.4 %fusion.93 = (bf16[256,2048]{1,0:T(8,128)(2,1)S(1)}, f32[256,2048]{1,0:T(8,128)S(1)}) fusion(bf16[256,2048]{1,0:T(8,128)(2,1)} %collective-permute-done.5, bf16[4096,2048]{1,0:T(8,128)(2,1)} %param.10, bf16[512,2048]{1,0:T(8,128)(2,1)S(1)} %get-tuple-element.23, s32[]{:T(128)S(6)} %select_n.136), kind=kOutput, calls=%fused_computation.146 | convolution fusion | flops 2150105088 | bytes 13631492 | tf_op jit(solution)/shard_map/dot_general | solution.py:145
  151.0 16.0 %collective-permute-done.16 = bf16[256,2048]{1,0:T(8,128)(2,1)} collective-permute-done((bf16[256,2048]{1,0:T(8,128)(2,1)}, bf16[256,2048]{1,0:T(8,128)(2,1)}, u32[]{:S(2)}, u32[]{:S(2)}) %collective-permute-start.16) | collective-permute-done | bytes 1048608 | tf_op jit(solution)/shard_map/ppermute | solution.py:156
  170.0 6.0 %fusion.92 = (bf16[256,2048]{1,0:T(8,128)(2,1)S(1)}, f32[256,2048]{1,0:T(8,128)S(1)}) fusion(bf16[256,2048]{1,0:T(8,128)(2,1)} %collective-permute-done.16, bf16[4096,2048]{1,0:T(8,128)(2,1)} %param.10, bf16[512,2048]{1,0:T(8,128)(2,1)S(1)} %get-tuple-element.23, s32[]{:T(128)S(6)} %select_n.136), kind=kOutput, calls=%fused_computation.145 | convolution fusion | flops 2150105088 | bytes 13631492 | tf_op jit(solution)/shard_map/dot_general | solution.py:145
  176.0 13.4 %collective-permute-done.2 = bf16[256,2048]{1,0:T(8,128)(2,1)S(1)} collective-permute-done((bf16[256,2048]{1,0:T(8,128)(2,1)}, bf16[256,2048]{1,0:T(8,128)(2,1)S(1)}, u32[]{:S(2)}, u32[]{:S(2)}) %collective-permute-start.2) | collective-permute-done | bytes 1048608 | tf_op jit(solution)/shard_map/ppermute | solution.py:156
  190.1 5.7 %fusion.18 = f32[256,2048]{1,0:T(8,128)S(1)} fusion(bf16[256,2048]{1,0:T(8,128)(2,1)S(1)} %collective-permute-done.2, bf16[4096,2048]{1,0:T(8,128)(2,1)} %param.10, bf16[512,2048]{1,0:T(8,128)(2,1)S(1)} %get-tuple-element.17, s32[]{:T(128)S(6)} %select_n.136), kind=kOutput, calls=%fused_computation.38 | convolution fusion | flops 2149580800 | bytes 12582916 | tf_op jit(solution)/shard_map/dot_general | solution.py:145
  195.9 16.0 %collective-permute-done.4 = bf16[256,2048]{1,0:T(8,128)(2,1)S(1)} collective-permute-done((bf16[256,2048]{1,0:T(8,128)(2,1)}, bf16[256,2048]{1,0:T(8,128)(2,1)S(1)}, u32[]{:S(2)}, u32[]{:S(2)}) %collective-permute-start.4) | collective-permute-done | bytes 1048608 | tf_op jit(solution)/shard_map/ppermute | solution.py:156
  214.8 5.7 %fusion.16 = f32[256,2048]{1,0:T(8,128)S(1)} fusion(bf16[256,2048]{1,0:T(8,128)(2,1)S(1)} %collective-permute-done.4, bf16[4096,2048]{1,0:T(8,128)(2,1)} %param.10, bf16[512,2048]{1,0:T(8,128)(2,1)S(1)} %get-tuple-element.22, s32[]{:T(128)S(6)} %select_n.136), kind=kOutput, calls=%fused_computation.34 | convolution fusion | flops 2149580800 | bytes 12582916 | tf_op jit(solution)/shard_map/dot_general | solution.py:145
  222.8 33.6 %collective-permute-done.14 = bf16[256,2048]{1,0:T(8,128)(2,1)S(1)} collective-permute-done((bf16[256,2048]{1,0:T(8,128)(2,1)}, bf16[256,2048]{1,0:T(8,128)(2,1)S(1)}, u32[]{:S(2)}, u32[]{:S(2)}) %collective-permute-start.14) | collective-permute-done | bytes 1048608 | tf_op jit(solution)/shard_map/ppermute | solution.py:156
  256.4 3.3 collective-permute-start.7
  259.7 5.7 %fusion.6 = f32[256,2048]{1,0:T(8,128)S(1)} fusion(bf16[256,2048]{1,0:T(8,128)(2,1)S(1)} %collective-permute-done.14, bf16[4096,2048]{1,0:T(8,128)(2,1)} %param.10, bf16[512,2048]{1,0:T(8,128)(2,1)S(1)} %get-tuple-element.17, s32[]{:T(128)S(6)} %select_n.136), kind=kOutput, calls=%fused_computation.18 | convolution fusion | flops 2149580800 | bytes 12582916 | tf_op jit(solution)/shard_map/dot_general | solution.py:145
  266.9 3.4 collective-permute-start.18
  271.2 12.0 %collective-permute-done.7 = bf16[256,2048]{1,0:T(8,128)(2,1)S(1)} collective-permute-done((bf16[256,2048]{1,0:T(8,128)(2,1)S(1)}, bf16[256,2048]{1,0:T(8,128)(2,1)S(1)}, u32[]{:S(2)}, u32[]{:S(2)}) %collective-permute-start.7) | collective-permute-done | bytes 1048608 | tf_op jit(solution)/shard_map/ppermute | solution.py:169
  286.2 4.1 %collective-permute-done.15 = bf16[256,2048]{1,0:T(8,128)(2,1)S(1)} collective-permute-done((bf16[256,2048]{1,0:T(8,128)(2,1)S(1)}, bf16[256,2048]{1,0:T(8,128)(2,1)S(1)}, u32[]{:S(2)}, u32[]{:S(2)}) %collective-permute-start.15) | collective-permute-done | bytes 1048608 | tf_op jit(solution)/shard_map/ppermute | solution.py:156
  290.3 4.3 %collective-permute-start.8 = (bf16[256,2048]{1,0:T(8,128)(2,1)S(1)}, bf16[256,2048]{1,0:T(8,128)(2,1)}, u32[]{:S(2)}, u32[]{:S(2)}) collective-permute-start(bf16[256,2048]{1,0:T(8,128)(2,1)S(1)} %get-tuple-element.12), channel_id=1, source_target_pairs={{0,4},{2,6},{4,8},{6,10},{8,12},{10,14},{1,5},{3,7},{5,9},{7,11},{... | collective-permute-start | bytes 3145736 | tf_op jit(solution)/shard_map/ppermute | solution.py:173
  294.7 5.7 %fusion.4 = f32[256,2048]{1,0:T(8,128)S(1)} fusion(bf16[256,2048]{1,0:T(8,128)(2,1)S(1)} %collective-permute-done.15, bf16[4096,2048]{1,0:T(8,128)(2,1)} %param.10, bf16[512,2048]{1,0:T(8,128)(2,1)S(1)} %get-tuple-element.22, s32[]{:T(128)S(6)} %select_n.136), kind=kOutput, calls=%fused_computation.14 | convolution fusion | flops 2149580800 | bytes 12582916 | tf_op jit(solution)/shard_map/dot_general | solution.py:145
  300.4 5.2 %collective-permute-done.18 = bf16[256,2048]{1,0:T(8,128)(2,1)S(1)} collective-permute-done((bf16[256,2048]{1,0:T(8,128)(2,1)S(1)}, bf16[256,2048]{1,0:T(8,128)(2,1)S(1)}, u32[]{:S(2)}, u32[]{:S(2)}) %collective-permute-start.18) | collective-permute-done | bytes 1048608 | tf_op jit(solution)/shard_map/ppermute | solution.py:169
  308.2 5.4 %collective-permute-start.19 = (bf16[256,2048]{1,0:T(8,128)(2,1)}, bf16[256,2048]{1,0:T(8,128)(2,1)}, u32[]{:S(2)}, u32[]{:S(2)}) collective-permute-start(bf16[256,2048]{1,0:T(8,128)(2,1)} %get-tuple-element.18), channel_id=1, source_target_pairs={{0,4},{2,6},{4,8},{6,10},{8,12},{10,14},{1,5},{3,7},{5,9},{7,11},{... | collective-permute-start | bytes 3145736 | tf_op jit(solution)/shard_map/ppermute | solution.py:173
  315.0 4.1 %fusion = bf16[8,16,4096]{2,0,1:T(8,128)(2,1)S(1)} fusion(bf16[16,16,4096]{2,1,0:T(8,128)(2,1)} %all-gather.2.cloned.1.call-done, s32[16]{0:T(128)S(1)} %gather_fusion.2, s32[8]{0:T(128)S(1)} %iota_add_fusion.1), kind=kOutput, calls=%fused_computation.4 | convolution fusion | flops 17825920 | bytes 3145824 | tf_op jit(solution)/shard_map/sb,brd->srd/dot_general | solution.py:223
  320.6 7.5 %collective-permute-done.8 = bf16[256,2048]{1,0:T(8,128)(2,1)} collective-permute-done((bf16[256,2048]{1,0:T(8,128)(2,1)S(1)}, bf16[256,2048]{1,0:T(8,128)(2,1)}, u32[]{:S(2)}, u32[]{:S(2)}) %collective-permute-start.8) | collective-permute-done | bytes 1048608 | tf_op jit(solution)/shard_map/ppermute | solution.py:173
  328.2 7.5 %fusion.24 = bf16[256,2048]{1,0:T(8,128)(2,1)S(1)} fusion(f32[256,4096]{1,0:T(8,128)S(1)} %bitcast.32, bf16[256,2048]{1,0:T(8,128)(2,1)} %collective-permute-done.11, bf16[256,2048]{1,0:T(8,128)(2,1)} %collective-permute-done.8, bf16[256,2048]{1,0:T(8,128)(2,1)} %collective-permute-done.1, bf16[4096,2048]{1,0:T(8,128)(2,1)} %param.10, ...), kind=kOutput, calls=%fused_computation.46 | convolution fusion | flops 2152726528 | bytes 15728644 | tf_op jit(solution)/shard_map/dot_general | solution.py:145
  335.7 14.0 %collective-permute-done.19 = bf16[256,2048]{1,0:T(8,128)(2,1)} collective-permute-done((bf16[256,2048]{1,0:T(8,128)(2,1)}, bf16[256,2048]{1,0:T(8,128)(2,1)}, u32[]{:S(2)}, u32[]{:S(2)}) %collective-permute-start.19) | collective-permute-done | bytes 1048608 | tf_op jit(solution)/shard_map/ppermute | solution.py:173
  349.7 7.3 %fusion.12 = bf16[256,2048]{1,0:T(8,128)(2,1)S(1)} fusion(f32[256,4096]{1,0:T(8,128)S(1)} %bitcast.33, bf16[256,2048]{1,0:T(8,128)(2,1)} %collective-permute-done.22, bf16[256,2048]{1,0:T(8,128)(2,1)} %collective-permute-done.19, bf16[256,2048]{1,0:T(8,128)(2,1)} %copy-done.7, bf16[4096,2048]{1,0:T(8,128)(2,1)} %param.10, ...), kind=kOutput, calls=%fused_computation.26 | convolution fusion | flops 2152726528 | bytes 15728644 | tf_op jit(solution)/shard_map/dot_general | solution.py:145
  (105 shorter events, 70.7 us)
Async XLA Ops:
  7.2 36.9 %copy-start = (bf16[256,4096]{1,0:T(8,128)(2,1)S(1)}, bf16[256,4096]{1,0:T(8,128)(2,1)}, u32[]{:S(2)}) copy-start(bf16[256,4096]{1,0:T(8,128)(2,1)} %param.8) | copy-start | bytes 6291460
  11.5 15.3 %copy-start.8 = (s32[16]{0:T(128)S(1)}, s32[16]{0:T(128)}, u32[]{:S(2)}) copy-start(s32[16]{0:T(128)} %param.13) | copy-start | bytes 196
  15.5 14.6 %all-to-all-start.1 = ((f32[8,32,128]{2,1,0:T(8,128)}), f32[8,32,128]{2,1,0:T(8,128)S(1)}, u32[]{:S(2)}, u32[]{:S(2)}) async-start(f32[8,32,128]{2,1,0:T(8,128)} %bitcast.8), calls=%async_computation.1 | async-start | bytes 262144 | tf_op jit(solution)/shard_map/all_to_all | solution.py:189
  30.2 13.6 %all-to-all-start = ((bf16[16,16,512]{2,1,0:T(8,128)(2,1)}), bf16[16,16,512]{2,1,0:T(8,128)(2,1)S(1)}, u32[]{:S(2)}, u32[]{:S(2)}) async-start(bf16[16,16,512]{2,1,0:T(8,128)(2,1)} %gather_fusion), calls=%async_computation | async-start | bytes 524288 | tf_op jit(solution)/shard_map/all_to_all | solution.py:180
  35.3 279.7 %all-gather.2.cloned.1.call-start = ((), (), s32[]{:S(2)}) async-start(), calls=%async_computation.2 | async-start | bytes 2359296 | tf_op jit(solution)/shard_map/all_gather | solution.py:219
  40.2 62.0 %collective-permute-start = (bf16[512,2048]{1,0:T(8,128)(2,1)}, bf16[512,2048]{1,0:T(8,128)(2,1)}, u32[]{:S(2)}, u32[]{:S(2)}) collective-permute-start(bf16[512,2048]{1,0:T(8,128)(2,1)} %get-tuple-element.24), channel_id=1, source_target_pairs={{0,1},{1,0},{2,3},{3,2},{4,5},{5,4},{6,7},{7,6},{8,9},{9,8},{10,11... | collective-permute-start | bytes 6291464 | tf_op jit(solution)/shard_map/ppermute | solution.py:137
  40.2 48.9 %collective-permute-start.3 = (bf16[512,2048]{1,0:T(8,128)(2,1)}, bf16[512,2048]{1,0:T(8,128)(2,1)}, u32[]{:S(2)}, u32[]{:S(2)}) collective-permute-start(bf16[512,2048]{1,0:T(8,128)(2,1)} %get-tuple-element.25), channel_id=1, source_target_pairs={{0,1},{1,0},{2,3},{3,2},{4,5},{5,4},{6,7},{7,6},{8,9},{9,8},{10,11... | collective-permute-start | bytes 6291464 | tf_op jit(solution)/shard_map/ppermute | solution.py:137
  44.8 2.6 collective-permute-start.12
  81.2 3.9 %collective-permute-start.23 = (bf16[8,16,2048]{2,1,0:T(8,128)(2,1)S(1)}, bf16[8,16,2048]{2,1,0:T(8,128)(2,1)S(1)}, u32[]{:S(2)}, u32[]{:S(2)}) collective-permute-start(bf16[8,16,2048]{2,1,0:T(8,128)(2,1)S(1)} %convolution_convert_fusion.17), channel_id=1, source_target_pairs={{0,1},{1,0},{2,3},{3,2},{4,5},{5,4},{6,7},{7,6},{8,9},{9,8},{10,11... | collective-permute-start | bytes 1572872 | tf_op jit(solution)/shard_map/ppermute | solution.py:230
  104.6 19.0 %copy-start.4 = (bf16[512,2048]{1,0:T(8,128)(2,1)}, bf16[512,2048]{1,0:T(8,128)(2,1)S(1)}, u32[]{:S(2)}) copy-start(bf16[512,2048]{1,0:T(8,128)(2,1)S(1)} %get-tuple-element.16) | copy-start | bytes 6291460
  118.3 26.3 %collective-permute-start.5 = (bf16[256,2048]{1,0:T(8,128)(2,1)}, bf16[256,2048]{1,0:T(8,128)(2,1)}, u32[]{:S(2)}, u32[]{:S(2)}) collective-permute-start(bf16[256,2048]{1,0:T(8,128)(2,1)} %convolution_convert_fusion.9), channel_id=1, source_target_pairs={{0,2},{2,0},{4,6},{6,4},{8,10},{10,8},{12,14},{14,12},{1,3},{3,1},... | collective-permute-start | bytes 3145736 | tf_op jit(solution)/shard_map/ppermute | solution.py:156
  121.6 45.4 %collective-permute-start.16 = (bf16[256,2048]{1,0:T(8,128)(2,1)}, bf16[256,2048]{1,0:T(8,128)(2,1)}, u32[]{:S(2)}, u32[]{:S(2)}) collective-permute-start(bf16[256,2048]{1,0:T(8,128)(2,1)} %convolution_convert_fusion.1), channel_id=1, source_target_pairs={{0,2},{2,0},{4,6},{6,4},{8,10},{10,8},{12,14},{14,12},{1,3},{3,1},... | collective-permute-start | bytes 3145736 | tf_op jit(solution)/shard_map/ppermute | solution.py:156
  127.0 62.4 %collective-permute-start.2 = (bf16[256,2048]{1,0:T(8,128)(2,1)}, bf16[256,2048]{1,0:T(8,128)(2,1)S(1)}, u32[]{:S(2)}, u32[]{:S(2)}) collective-permute-start(bf16[256,2048]{1,0:T(8,128)(2,1)} %convolution_convert_fusion.13), channel_id=1, source_target_pairs={{0,2},{2,0},{4,6},{6,4},{8,10},{10,8},{12,14},{14,12},{1,3},{3,1},... | collective-permute-start | bytes 3145736 | tf_op jit(solution)/shard_map/ppermute | solution.py:156
  127.0 84.9 %collective-permute-start.4 = (bf16[256,2048]{1,0:T(8,128)(2,1)}, bf16[256,2048]{1,0:T(8,128)(2,1)S(1)}, u32[]{:S(2)}, u32[]{:S(2)}) collective-permute-start(bf16[256,2048]{1,0:T(8,128)(2,1)} %convolution_convert_fusion.11), channel_id=1, source_target_pairs={{0,2},{2,0},{4,6},{6,4},{8,10},{10,8},{12,14},{14,12},{1,3},{3,1},... | collective-permute-start | bytes 3145736 | tf_op jit(solution)/shard_map/ppermute | solution.py:156
  129.0 184.7 %collective-permute-start.1 = (bf16[256,2048]{1,0:T(8,128)(2,1)}, bf16[256,2048]{1,0:T(8,128)(2,1)}, u32[]{:S(2)}, u32[]{:S(2)}) collective-permute-start(bf16[256,2048]{1,0:T(8,128)(2,1)} %convolution_convert_fusion.15), channel_id=1, source_target_pairs={{0,2},{2,0},{4,6},{6,4},{8,10},{10,8},{12,14},{14,12},{1,3},{3,1},... | collective-permute-start | bytes 3145736 | tf_op jit(solution)/shard_map/ppermute | solution.py:156
  144.5 111.9 %collective-permute-start.14 = (bf16[256,2048]{1,0:T(8,128)(2,1)}, bf16[256,2048]{1,0:T(8,128)(2,1)S(1)}, u32[]{:S(2)}, u32[]{:S(2)}) collective-permute-start(bf16[256,2048]{1,0:T(8,128)(2,1)} %convolution_convert_fusion.5), channel_id=1, source_target_pairs={{0,2},{2,0},{4,6},{6,4},{8,10},{10,8},{12,14},{14,12},{1,3},{3,1},... | collective-permute-start | bytes 3145736 | tf_op jit(solution)/shard_map/ppermute | solution.py:156
  167.0 53.6 %collective-permute-start.6 = (bf16[256,2048]{1,0:T(8,128)(2,1)S(1)}, bf16[256,2048]{1,0:T(8,128)(2,1)S(1)}, u32[]{:S(2)}, u32[]{:S(2)}) collective-permute-start(bf16[256,2048]{1,0:T(8,128)(2,1)S(1)} %get-tuple-element.34), channel_id=1, source_target_pairs={{0,4},{2,6},{1,5},{3,7},{16,20},{18,22},{17,21},{19,23}} | collective-permute-start | bytes 3145736 | tf_op jit(solution)/shard_map/ppermute | solution.py:165
  189.4 32.0 %collective-permute-start.9 = (bf16[256,2048]{1,0:T(8,128)(2,1)S(1)}, bf16[256,2048]{1,0:T(8,128)(2,1)S(1)}, u32[]{:S(2)}, u32[]{:S(2)}) collective-permute-start(bf16[256,2048]{1,0:T(8,128)(2,1)S(1)} %get-tuple-element.34), channel_id=1, source_target_pairs={{14,10},{12,8},{15,11},{13,9},{30,26},{28,24},{31,27},{29,25}} | collective-permute-start | bytes 3145736 | tf_op jit(solution)/shard_map/ppermute | solution.py:166
  211.8 53.7 %collective-permute-start.17 = (bf16[256,2048]{1,0:T(8,128)(2,1)S(1)}, bf16[256,2048]{1,0:T(8,128)(2,1)S(1)}, u32[]{:S(2)}, u32[]{:S(2)}) collective-permute-start(bf16[256,2048]{1,0:T(8,128)(2,1)S(1)} %get-tuple-element.32), channel_id=1, source_target_pairs={{0,4},{2,6},{1,5},{3,7},{16,20},{18,22},{17,21},{19,23}} | collective-permute-start | bytes 3145736 | tf_op jit(solution)/shard_map/ppermute | solution.py:165
  220.6 45.6 %collective-permute-start.20 = (bf16[256,2048]{1,0:T(8,128)(2,1)S(1)}, bf16[256,2048]{1,0:T(8,128)(2,1)S(1)}, u32[]{:S(2)}, u32[]{:S(2)}) collective-permute-start(bf16[256,2048]{1,0:T(8,128)(2,1)S(1)} %get-tuple-element.32), channel_id=1, source_target_pairs={{14,10},{12,8},{15,11},{13,9},{30,26},{28,24},{31,27},{29,25}} | collective-permute-start | bytes 3145736 | tf_op jit(solution)/shard_map/ppermute | solution.py:166
  222.1 48.2 %collective-permute-start.10 = (bf16[256,2048]{1,0:T(8,128)(2,1)S(1)}, bf16[256,2048]{1,0:T(8,128)(2,1)S(1)}, u32[]{:S(2)}, u32[]{:S(2)}) collective-permute-start(bf16[256,2048]{1,0:T(8,128)(2,1)S(1)} %get-tuple-element.15), channel_id=1, source_target_pairs={{14,10},{12,8},{10,6},{8,4},{15,11},{13,9},{11,7},{9,5},{30,26},{2... | collective-permute-start | bytes 3145736 | tf_op jit(solution)/shard_map/ppermute | solution.py:170
  256.4 26.8 %collective-permute-start.7 = (bf16[256,2048]{1,0:T(8,128)(2,1)S(1)}, bf16[256,2048]{1,0:T(8,128)(2,1)S(1)}, u32[]{:S(2)}, u32[]{:S(2)}) collective-permute-start(bf16[256,2048]{1,0:T(8,128)(2,1)S(1)} %get-tuple-element.14), channel_id=1, source_target_pairs={{0,4},{2,6},{4,8},{6,10},{1,5},{3,7},{5,9},{7,11},{16,20},{18,22},... | collective-permute-start | bytes 3145736 | tf_op jit(solution)/shard_map/ppermute | solution.py:169
  265.5 24.8 %collective-permute-start.15 = (bf16[256,2048]{1,0:T(8,128)(2,1)S(1)}, bf16[256,2048]{1,0:T(8,128)(2,1)S(1)}, u32[]{:S(2)}, u32[]{:S(2)}) collective-permute-start(bf16[256,2048]{1,0:T(8,128)(2,1)S(1)} %copy-done.6), channel_id=1, source_target_pairs={{0,2},{2,0},{4,6},{6,4},{8,10},{10,8},{12,14},{14,12},{1,3},{3,1},... | collective-permute-start | bytes 3145736 | tf_op jit(solution)/shard_map/ppermute | solution.py:156
  266.9 38.8 %collective-permute-start.18 = (bf16[256,2048]{1,0:T(8,128)(2,1)S(1)}, bf16[256,2048]{1,0:T(8,128)(2,1)S(1)}, u32[]{:S(2)}, u32[]{:S(2)}) collective-permute-start(bf16[256,2048]{1,0:T(8,128)(2,1)S(1)} %get-tuple-element.20), channel_id=1, source_target_pairs={{0,4},{2,6},{4,8},{6,10},{1,5},{3,7},{5,9},{7,11},{16,20},{18,22},... | collective-permute-start | bytes 3145736 | tf_op jit(solution)/shard_map/ppermute | solution.py:169
  270.3 35.9 %collective-permute-start.21 = (bf16[256,2048]{1,0:T(8,128)(2,1)S(1)}, bf16[256,2048]{1,0:T(8,128)(2,1)S(1)}, u32[]{:S(2)}, u32[]{:S(2)}) collective-permute-start(bf16[256,2048]{1,0:T(8,128)(2,1)S(1)} %get-tuple-element.21), channel_id=1, source_target_pairs={{14,10},{12,8},{10,6},{8,4},{15,11},{13,9},{11,7},{9,5},{30,26},{2... | collective-permute-start | bytes 3145736 | tf_op jit(solution)/shard_map/ppermute | solution.py:170
  284.9 35.7 %collective-permute-start.11 = (bf16[256,2048]{1,0:T(8,128)(2,1)}, bf16[256,2048]{1,0:T(8,128)(2,1)}, u32[]{:S(2)}, u32[]{:S(2)}) collective-permute-start(bf16[256,2048]{1,0:T(8,128)(2,1)} %get-tuple-element.13), channel_id=1, source_target_pairs={{14,10},{12,8},{10,6},{8,4},{6,2},{4,0},{15,11},{13,9},{11,7},{9,5... | collective-permute-start | bytes 3145736 | tf_op jit(solution)/shard_map/ppermute | solution.py:174
  290.3 37.8 %collective-permute-start.8 = (bf16[256,2048]{1,0:T(8,128)(2,1)S(1)}, bf16[256,2048]{1,0:T(8,128)(2,1)}, u32[]{:S(2)}, u32[]{:S(2)}) collective-permute-start(bf16[256,2048]{1,0:T(8,128)(2,1)S(1)} %get-tuple-element.12), channel_id=1, source_target_pairs={{0,4},{2,6},{4,8},{6,10},{8,12},{10,14},{1,5},{3,7},{5,9},{7,11},{... | collective-permute-start | bytes 3145736 | tf_op jit(solution)/shard_map/ppermute | solution.py:173
  305.7 30.0 %collective-permute-start.13 = (bf16[256,2048]{1,0:T(8,128)(2,1)}, bf16[256,2048]{1,0:T(8,128)(2,1)S(1)}, u32[]{:S(2)}, u32[]{:S(2)}) collective-permute-start(bf16[256,2048]{1,0:T(8,128)(2,1)} %convolution_convert_fusion.7), channel_id=1, source_target_pairs={{0,2},{2,0},{4,6},{6,4},{8,10},{10,8},{12,14},{14,12},{1,3},{3,1},... | collective-permute-start | bytes 3145736 | tf_op jit(solution)/shard_map/ppermute | solution.py:156
  308.2 41.5 %collective-permute-start.19 = (bf16[256,2048]{1,0:T(8,128)(2,1)}, bf16[256,2048]{1,0:T(8,128)(2,1)}, u32[]{:S(2)}, u32[]{:S(2)}) collective-permute-start(bf16[256,2048]{1,0:T(8,128)(2,1)} %get-tuple-element.18), channel_id=1, source_target_pairs={{0,4},{2,6},{4,8},{6,10},{8,12},{10,14},{1,5},{3,7},{5,9},{7,11},{... | collective-permute-start | bytes 3145736 | tf_op jit(solution)/shard_map/ppermute | solution.py:173
  313.6 36.1 %collective-permute-start.22 = (bf16[256,2048]{1,0:T(8,128)(2,1)}, bf16[256,2048]{1,0:T(8,128)(2,1)}, u32[]{:S(2)}, u32[]{:S(2)}) collective-permute-start(bf16[256,2048]{1,0:T(8,128)(2,1)} %get-tuple-element.19), channel_id=1, source_target_pairs={{14,10},{12,8},{10,6},{8,4},{6,2},{4,0},{15,11},{13,9},{11,7},{9,5... | collective-permute-start | bytes 3145736 | tf_op jit(solution)/shard_map/ppermute | solution.py:174
  328.2 21.6 %copy-start.5 = (bf16[512,2048]{1,0:T(8,128)(2,1)S(1)}, bf16[512,2048]{1,0:T(8,128)(2,1)}, u32[]{:S(2)}) copy-start(bf16[512,2048]{1,0:T(8,128)(2,1)} %copy-done.4) | copy-start | bytes 6291460
  335.7 14.0 %copy-start.7 = (bf16[256,2048]{1,0:T(8,128)(2,1)}, bf16[256,2048]{1,0:T(8,128)(2,1)S(1)}, u32[]{:S(2)}) copy-start(bf16[256,2048]{1,0:T(8,128)(2,1)S(1)} %collective-permute-done.13) | copy-start | bytes 3145732
  (8 other events, 73.5 us)
Sparse Core Ops, SparseCore 0:
  82.5 51.7 all-gather.1
